TPU v7x, 32 devices: a whole 2x2x4 slice. The times are simulated.
32 devices in a mesh: blk: 32 (over z, y, x, core).
Axes of the slice: x: 2, y: 2, z: 4, core: 2. Of those that a mesh axis runs over, the one named last changes fastest.
Arguments:
- raw_tiles: bfloat16 [256, 64, 384], P('blk'), may hold values from -6 to 6
- flat_field: bfloat16 [32, 64, 384], P('blk'), may hold values from 0.5 to 2
- dark_field: bfloat16 [32, 64, 384], P('blk'), may hold values from -3 to 3
- blend_ramp: int32 [32, 384], P('blk'), may hold values from 1 to 65
- source_used: int32 [32, 5], P('blk'), may hold values from 0 to 1, as said below
- source_offset: int32 [32, 5], P('blk'), may hold values from 0 to 128
Outputs:
- volume: float32 [256, 64, 256], P('blk')
Inputs may be any that keep to these rules, and one draw needn't show every extreme that they name: source_used[b, 2] is 1 for every block, and no used slot names a tile outside 0..31.
All inputs are finite; a program needn't handle non-finite values.
Results may differ from a plain program's by a relative error of at most 0.0003.
Values may be sent and summed in bfloat16 or wider, within the bound.
A program may use at most 64 MiB of HBM per device.

v0:
```python
import jax
import jax.numpy as jnp
from jax import lax
from jax.sharding import PartitionSpec as P

BX = 256


thresholds = (1.0, 0.8, 0.6, 0.5)


def passed_along(block, axis, distance):
    devices = range(lax.axis_size(axis))
    route = [(i - distance, i) for i in devices if i - distance in devices]
    return lax.ppermute(block, axis, route)


def padded_2(array, sides, width):
    for axis, dim in sides:
        devices, length = (lax.axis_size(axis), array.shape[dim])
        up = [(i, (i + 1) % devices) for i in range(devices - 1)]
        down = [(j, i) for i, j in up]
        last = lax.slice_in_dim(array, length - width, length, axis=dim)
        leading = lax.slice_in_dim(array, 0, width, axis=dim)
        before = lax.ppermute(last, axis, up)
        after = lax.ppermute(leading, axis, down)
        array = jnp.concatenate([before, array, after], axis=dim)
    return array


def correct(camera, flat_gain, dark_level):
    return (camera.astype(jnp.float32) - dark_level.astype(jnp.float32)[None]) / flat_gain.astype(
        jnp.float32
    )[None]


def diffuse(extended, kappa_value):
    padded = jnp.pad(extended, ((0, 0), (1, 1), (1, 1)), mode="edge")
    center = padded[1:-1, 1:-1, 1:-1]
    others = [
        padded[2:, 1:-1, 1:-1],
        padded[:-2, 1:-1, 1:-1],
        padded[1:-1, 2:, 1:-1],
        padded[1:-1, :-2, 1:-1],
        padded[1:-1, 1:-1, 2:],
        padded[1:-1, 1:-1, :-2],
    ]
    flux_sum = jnp.zeros(center.shape, jnp.float32)
    for neighbour in others:
        gradient = neighbour - center
        scaled = gradient / kappa_value
        flux_sum = flux_sum + gradient / (1.0 + scaled * scaled)
    return center + 0.12 * flux_sum


def pin_edges(extended, depth, is_first, is_last):
    size_z = extended.shape[0]
    rest = extended.shape[1:]
    lower = jnp.broadcast_to(extended[depth : depth + 1], (depth,) + rest)
    upper = jnp.broadcast_to(extended[size_z - depth - 1 : size_z - depth], (depth,) + rest)
    extended = extended.at[:depth].set(jnp.where(is_first, lower, extended[:depth]))
    extended = extended.at[size_z - depth :].set(
        jnp.where(is_last, upper, extended[size_z - depth :])
    )
    return extended


def shards(raw_tiles, flat_field, dark_field, blend_ramp, source_used, source_offset):
    flat_gain = flat_field[0]
    dark_level = dark_field[0]
    used_row = source_used[0]
    offset_row = source_offset[0]
    numerator = jnp.zeros((raw_tiles.shape[0], raw_tiles.shape[1], BX), jnp.float32)
    denominator = jnp.zeros((BX,), jnp.float32)
    own_tile = correct(raw_tiles, flat_gain, dark_level)
    own_weights = blend_ramp[0].astype(jnp.float32)
    for slot_id in range(5):
        step_delta = slot_id - 2
        offset = offset_row[slot_id]
        if step_delta == 0:
            corrected, weights_all = (own_tile, own_weights)
        else:
            corrected, weights_all = passed_along((own_tile, own_weights), "blk", -step_delta)
        window = lax.dynamic_slice_in_dim(corrected, offset, BX, 2)
        weights = lax.dynamic_slice_in_dim(weights_all, offset, BX, 0)
        taken = used_row[slot_id] == 1
        numerator = numerator + jnp.where(taken, window * weights, jnp.float32(0.0))
        denominator = denominator + jnp.where(taken, weights, jnp.float32(0.0))
    volume = numerator / denominator
    position = lax.axis_index("blk")
    is_first = position == 0
    is_last = position == lax.axis_size("blk") - 1
    for pair_index in range(len(thresholds) // 2):
        extended = padded_2(volume, (("blk", 0),), 2)
        middle_section = diffuse(
            pin_edges(extended, 2, is_first, is_last), thresholds[2 * pair_index]
        )
        middle_section = pin_edges(middle_section, 1, is_first, is_last)
        volume = diffuse(middle_section, thresholds[2 * pair_index + 1])
    return volume


def solution(mesh):
    return jax.shard_map(
        shards,
        mesh=mesh,
        in_specs=(
            P("blk", None, None),
            P("blk", None, None),
            P("blk", None, None),
            P("blk", None),
            P("blk", None),
            P("blk", None),
        ),
        out_specs=P("blk", None, None),
        check_vma=False,
    )
```

profile of v0, /device:TPU:7, one launch (start us, length us, event | category | flops | bytes accessed | tf_op | source)
XLA Modules:
  0.0 110.8 jit_solution(13966596679365641483)
XLA Ops:
  0.0 0.8 bitcast_convert_fusion
  0.8 0.0 copy-start.2
  0.9 1.1 subtract_divide_fusion
  1.9 3.1 %collective-permute-start = (f32[8,64,384]{2,1,0:T(8,128)S(1)}, f32[8,64,384]{2,1,0:T(8,128)S(1)}, u32[]{:S(2)}, u32[]{:S(2)}) collective-permute-start(f32[8,64,384]{2,1,0:T(8,128)S(1)} %subtract_divide_fusion), channel_id=1, source_target_pairs={{0,2},{1,3},{2,4},{3,5},{4,6},{5,7},{6,8},{7,9},{8,10},{9,11},{10,... | collective-permute-start | bytes 2359304 | tf_op jit(solution)/shard_map/ppermute | solution.py:15
  5.1 4.0 %collective-permute-start.2 = (f32[8,64,384]{2,1,0:T(8,128)S(1)}, f32[8,64,384]{2,1,0:T(8,128)S(1)}, u32[]{:S(2)}, u32[]{:S(2)}) collective-permute-start(f32[8,64,384]{2,1,0:T(8,128)S(1)} %subtract_divide_fusion), channel_id=1, source_target_pairs={{0,1},{1,2},{2,3},{3,4},{4,5},{5,6},{6,7},{7,8},{8,9},{9,10},{10,1... | collective-permute-start | bytes 2359304 | tf_op jit(solution)/shard_map/ppermute | solution.py:15
  9.0 1.9 %collective-permute-start.4 = (f32[8,64,384]{2,1,0:T(8,128)S(1)}, f32[8,64,384]{2,1,0:T(8,128)S(1)}, u32[]{:S(2)}, u32[]{:S(2)}) collective-permute-start(f32[8,64,384]{2,1,0:T(8,128)S(1)} %subtract_divide_fusion), channel_id=1, source_target_pairs={{1,0},{2,1},{3,2},{4,3},{5,4},{6,5},{7,6},{8,7},{9,8},{10,9},{11,1... | collective-permute-start | bytes 2359304 | tf_op jit(solution)/shard_map/ppermute | solution.py:15
  11.0 2.2 %collective-permute-start.6 = (f32[8,64,384]{2,1,0:T(8,128)S(1)}, f32[8,64,384]{2,1,0:T(8,128)}, u32[]{:S(2)}, u32[]{:S(2)}) collective-permute-start(f32[8,64,384]{2,1,0:T(8,128)S(1)} %subtract_divide_fusion), channel_id=1, source_target_pairs={{2,0},{3,1},{4,2},{5,3},{6,4},{7,5},{8,6},{9,7},{10,8},{11,9},{12,... | collective-permute-start | bytes 2359304 | tf_op jit(solution)/shard_map/ppermute | solution.py:15
  13.2 0.0 copy-start
  13.2 4.9 %collective-permute-start.1 = (f32[384]{0:T(512)S(1)}, f32[384]{0:T(512)S(1)}, u32[]{:S(2)}, u32[]{:S(2)}) collective-permute-start(f32[384]{0:T(512)S(1)} %convert_reduce_fusion), channel_id=1, source_target_pairs={{0,2},{1,3},{2,4},{3,5},{4,6},{5,7},{6,8},{7,9},{8,10},{9,11},{10,... | collective-permute-start | bytes 4616 | tf_op jit(solution)/shard_map/ppermute | solution.py:15
  18.1 0.0 copy-start.1
  18.1 0.7 fusion.33
  18.8 36.9 %collective-permute-done.1 = f32[384]{0:T(512)S(1)} collective-permute-done((f32[384]{0:T(512)S(1)}, f32[384]{0:T(512)S(1)}, u32[]{:S(2)}, u32[]{:S(2)}) %collective-permute-start.1) | collective-permute-done | bytes 1568 | tf_op jit(solution)/shard_map/ppermute | solution.py:15
  55.7 1.9 %collective-permute-start.3 = (f32[384]{0:T(512)S(1)}, f32[384]{0:T(512)S(1)}, u32[]{:S(2)}, u32[]{:S(2)}) collective-permute-start(f32[384]{0:T(512)S(1)} %convert_reduce_fusion), channel_id=1, source_target_pairs={{0,1},{1,2},{2,3},{3,4},{4,5},{5,6},{6,7},{7,8},{8,9},{9,10},{10,1... | collective-permute-start | bytes 4616 | tf_op jit(solution)/shard_map/ppermute | solution.py:15
  57.6 0.7 fusion.32
  60.2 0.0 collective-permute-done.3
  60.2 4.1 %collective-permute-start.5 = (f32[384]{0:T(512)S(1)}, f32[384]{0:T(512)S(1)}, u32[]{:S(2)}, u32[]{:S(2)}) collective-permute-start(f32[384]{0:T(512)S(1)} %convert_reduce_fusion), channel_id=1, source_target_pairs={{1,0},{2,1},{3,2},{4,3},{5,4},{6,5},{7,6},{8,7},{9,8},{10,9},{11,1... | collective-permute-start | bytes 4616 | tf_op jit(solution)/shard_map/ppermute | solution.py:15
  64.3 0.1 constant_dynamic-slice_fusion
  66.4 0.5 collective-permute-done.5
  66.9 3.5 %collective-permute-start.7 = (f32[384]{0:T(512)S(1)}, f32[384]{0:T(512)S(1)}, u32[]{:S(2)}, u32[]{:S(2)}) collective-permute-start(f32[384]{0:T(512)S(1)} %convert_reduce_fusion), channel_id=1, source_target_pairs={{2,0},{3,1},{4,2},{5,3},{6,4},{7,5},{8,6},{9,7},{10,8},{11,9},{12,... | collective-permute-start | bytes 4616 | tf_op jit(solution)/shard_map/ppermute | solution.py:15
  79.2 0.0 collective-permute-done.7
  79.3 0.1 select_add_fusion
  79.4 0.0 collective-permute-done
  79.4 0.0 collective-permute-done.2
  79.4 0.0 collective-permute-done.4
  79.4 0.0 collective-permute-done.6
  79.4 1.9 %add_divide_fusion = f32[8,64,256]{2,1,0:T(8,128)S(1)} fusion(f32[8,64,384]{2,1,0:T(8,128)} %collective-permute-done.6, s32[]{:T(128)S(6)} %select_n.141, f32[8,64,384]{2,1,0:T(8,128)S(1)} %collective-permute-done.4, s32[]{:T(128)S(6)} %select_n.138, f32[8,64,384]{2,1,0:T(8,128)S(1)} %subtract_divide_fusion, s32[]{:T(128)S(6)} %select_n.135, ...), kind=kLoop, calls=%fused_computation.67 | loop fusion | flops 1966080 | bytes 3151897 | tf_op jit(solution)/shard_map/div | solution.py:89
  81.3 4.6 %collective-permute-start.8 = (f32[2,64,256]{2,1,0:T(8,128)S(1)}, f32[2,64,256]{2,1,0:T(8,128)S(1)}, u32[]{:S(2)}, u32[]{:S(2)}) collective-permute-start(f32[2,64,256]{2,1,0:T(8,128)S(1)} %get-tuple-element.128), channel_id=1, source_target_pairs={{0,1},{1,2},{2,3},{3,4},{4,5},{5,6},{6,7},{7,8},{8,9},{9,10},{10,1... | collective-permute-start | bytes 393224 | tf_op jit(solution)/shard_map/ppermute | solution.py:25
  86.0 1.9 %collective-permute-start.9 = (f32[2,64,256]{2,1,0:T(8,128)S(1)}, f32[2,64,256]{2,1,0:T(8,128)S(1)}, u32[]{:S(2)}, u32[]{:S(2)}) collective-permute-start(f32[2,64,256]{2,1,0:T(8,128)S(1)} %get-tuple-element.129), channel_id=1, source_target_pairs={{1,0},{2,1},{3,2},{4,3},{5,4},{6,5},{7,6},{8,7},{9,8},{10,9},{11,1... | collective-permute-start | bytes 393224 | tf_op jit(solution)/shard_map/ppermute | solution.py:26
  87.9 0.0 collective-permute-done.8
  87.9 6.1 %collective-permute-done.9 = f32[2,64,256]{2,1,0:T(8,128)S(1)} collective-permute-done((f32[2,64,256]{2,1,0:T(8,128)S(1)}, f32[2,64,256]{2,1,0:T(8,128)S(1)}, u32[]{:S(2)}, u32[]{:S(2)}) %collective-permute-start.9) | collective-permute-done | bytes 131104 | tf_op jit(solution)/shard_map/ppermute | solution.py:26
  94.1 0.1 pad_maximum_fusion.2
  94.2 0.1 pad_maximum_fusion
  94.3 0.2 fusion.23
  94.5 1.1 multiply_add_fusion.1
  95.7 0.1 pad_maximum_fusion.4
  95.8 0.2 fusion.27
  96.0 1.0 multiply_add_fusion.3
  97.0 1.9 %collective-permute-start.10 = (f32[2,64,256]{2,1,0:T(8,128)S(1)}, f32[2,64,256]{2,1,0:T(8,128)S(1)}, u32[]{:S(2)}, u32[]{:S(2)}) collective-permute-start(f32[2,64,256]{2,1,0:T(8,128)S(1)} %get-tuple-element.124), channel_id=1, source_target_pairs={{0,1},{1,2},{2,3},{3,4},{4,5},{5,6},{6,7},{7,8},{8,9},{9,10},{10,1... | collective-permute-start | bytes 393224 | tf_op jit(solution)/shard_map/ppermute | solution.py:25
  98.9 2.4 %collective-permute-start.11 = (f32[2,64,256]{2,1,0:T(8,128)S(1)}, f32[2,64,256]{2,1,0:T(8,128)S(1)}, u32[]{:S(2)}, u32[]{:S(2)}) collective-permute-start(f32[2,64,256]{2,1,0:T(8,128)S(1)} %get-tuple-element.125), channel_id=1, source_target_pairs={{1,0},{2,1},{3,2},{4,3},{5,4},{6,5},{7,6},{8,7},{9,8},{10,9},{11,1... | collective-permute-start | bytes 393224 | tf_op jit(solution)/shard_map/ppermute | solution.py:26
  101.3 0.0 collective-permute-done.10
  101.3 5.6 %collective-permute-done.11 = f32[2,64,256]{2,1,0:T(8,128)S(1)} collective-permute-done((f32[2,64,256]{2,1,0:T(8,128)S(1)}, f32[2,64,256]{2,1,0:T(8,128)S(1)}, u32[]{:S(2)}, u32[]{:S(2)}) %collective-permute-start.11) | collective-permute-done | bytes 131104 | tf_op jit(solution)/shard_map/ppermute | solution.py:26
  107.0 0.1 pad_maximum_fusion.3
  107.1 0.1 pad_maximum_fusion.1
  107.2 0.2 fusion.22
  107.4 1.2 %multiply_add_fusion = f32[10,64,256]{2,1,0:T(8,128)S(1)} fusion(f32[12,1,256]{2,1,0:T(1,128)S(1)} %get-tuple-element.111, f32[12,64,256]{2,1,0:T(8,128)S(1)} %fusion.16, f32[12,1,256]{2,1,0:T(1,128)S(1)} %get-tuple-element.110, f32[12,66,1]{2,1,0:T(8,128)S(1)} %get-tuple-element.107, f32[12,66,1]{2,1,0:T(8,128)S(1)} %get-tuple-element.106), kind=kLoop, calls=%fused_computation.35 | loop fusion | flops 7372800 | bytes 4317184 | tf_op jit(solution)/shard_map/add | solution.py:53
  108.8 0.1 pad_maximum_fusion.5
  108.8 0.2 fusion.26
  109.0 1.8 %multiply_add_fusion.2 = f32[8,64,256]{2,1,0:T(8,128)} fusion(f32[10,1,256]{2,1,0:T(1,128)S(1)} %get-tuple-element.119, f32[10,64,256]{2,1,0:T(8,128)S(1)} %fusion.18, f32[10,1,256]{2,1,0:T(1,128)S(1)} %get-tuple-element.118, f32[10,66,1]{2,1,0:T(8,128)S(1)} %get-tuple-element.115, f32[10,66,1]{2,1,0:T(8,128)S(1)} %get-tuple-element.114), kind=kLoop, calls=%fused_computation.65 | loop fusion | flops 5898240 | bytes 3510272 | tf_op jit(solution)/shard_map/add | solution.py:53
  (25 shorter events, 0.4 us)
Async XLA Ops:
  0.8 12.3 %copy-start.2 = (s32[1,384]{1,0:T(1,128)S(1)}, s32[1,384]{1,0:T(1,128)}, u32[]{:S(2)}) copy-start(s32[1,384]{1,0:T(1,128)} %param.25) | copy-start | bytes 4612
  1.9 77.4 %collective-permute-start = (f32[8,64,384]{2,1,0:T(8,128)S(1)}, f32[8,64,384]{2,1,0:T(8,128)S(1)}, u32[]{:S(2)}, u32[]{:S(2)}) collective-permute-start(f32[8,64,384]{2,1,0:T(8,128)S(1)} %subtract_divide_fusion), channel_id=1, source_target_pairs={{0,2},{1,3},{2,4},{3,5},{4,6},{5,7},{6,8},{7,9},{8,10},{9,11},{10,... | collective-permute-start | bytes 2359304 | tf_op jit(solution)/shard_map/ppermute | solution.py:15
  5.1 74.3 %collective-permute-start.2 = (f32[8,64,384]{2,1,0:T(8,128)S(1)}, f32[8,64,384]{2,1,0:T(8,128)S(1)}, u32[]{:S(2)}, u32[]{:S(2)}) collective-permute-start(f32[8,64,384]{2,1,0:T(8,128)S(1)} %subtract_divide_fusion), channel_id=1, source_target_pairs={{0,1},{1,2},{2,3},{3,4},{4,5},{5,6},{6,7},{7,8},{8,9},{9,10},{10,1... | collective-permute-start | bytes 2359304 | tf_op jit(solution)/shard_map/ppermute | solution.py:15
  9.0 70.3 %collective-permute-start.4 = (f32[8,64,384]{2,1,0:T(8,128)S(1)}, f32[8,64,384]{2,1,0:T(8,128)S(1)}, u32[]{:S(2)}, u32[]{:S(2)}) collective-permute-start(f32[8,64,384]{2,1,0:T(8,128)S(1)} %subtract_divide_fusion), channel_id=1, source_target_pairs={{1,0},{2,1},{3,2},{4,3},{5,4},{6,5},{7,6},{8,7},{9,8},{10,9},{11,1... | collective-permute-start | bytes 2359304 | tf_op jit(solution)/shard_map/ppermute | solution.py:15
  11.0 68.4 %collective-permute-start.6 = (f32[8,64,384]{2,1,0:T(8,128)S(1)}, f32[8,64,384]{2,1,0:T(8,128)}, u32[]{:S(2)}, u32[]{:S(2)}) collective-permute-start(f32[8,64,384]{2,1,0:T(8,128)S(1)} %subtract_divide_fusion), channel_id=1, source_target_pairs={{2,0},{3,1},{4,2},{5,3},{6,4},{7,5},{8,6},{9,7},{10,8},{11,9},{12,... | collective-permute-start | bytes 2359304 | tf_op jit(solution)/shard_map/ppermute | solution.py:15
  13.2 5.0 %copy-start = (s32[1,5]{1,0:T(1,128)S(1)}, s32[1,5]{1,0:T(1,128)}, u32[]{:S(2)}) copy-start(s32[1,5]{1,0:T(1,128)} %param.27) | copy-start | bytes 64
  13.2 42.5 %collective-permute-start.1 = (f32[384]{0:T(512)S(1)}, f32[384]{0:T(512)S(1)}, u32[]{:S(2)}, u32[]{:S(2)}) collective-permute-start(f32[384]{0:T(512)S(1)} %convert_reduce_fusion), channel_id=1, source_target_pairs={{0,2},{1,3},{2,4},{3,5},{4,6},{5,7},{6,8},{7,9},{8,10},{9,11},{10,... | collective-permute-start | bytes 4616 | tf_op jit(solution)/shard_map/ppermute | solution.py:15
  18.1 39.5 %copy-start.1 = (s32[1,5]{1,0:T(1,128)S(1)}, s32[1,5]{1,0:T(1,128)}, u32[]{:S(2)}) copy-start(s32[1,5]{1,0:T(1,128)} %param.26) | copy-start | bytes 64
  55.7 4.5 %collective-permute-start.3 = (f32[384]{0:T(512)S(1)}, f32[384]{0:T(512)S(1)}, u32[]{:S(2)}, u32[]{:S(2)}) collective-permute-start(f32[384]{0:T(512)S(1)} %convert_reduce_fusion), channel_id=1, source_target_pairs={{0,1},{1,2},{2,3},{3,4},{4,5},{5,6},{6,7},{7,8},{8,9},{9,10},{10,1... | collective-permute-start | bytes 4616 | tf_op jit(solution)/shard_map/ppermute | solution.py:15
  60.2 6.7 %collective-permute-start.5 = (f32[384]{0:T(512)S(1)}, f32[384]{0:T(512)S(1)}, u32[]{:S(2)}, u32[]{:S(2)}) collective-permute-start(f32[384]{0:T(512)S(1)} %convert_reduce_fusion), channel_id=1, source_target_pairs={{1,0},{2,1},{3,2},{4,3},{5,4},{6,5},{7,6},{8,7},{9,8},{10,9},{11,1... | collective-permute-start | bytes 4616 | tf_op jit(solution)/shard_map/ppermute | solution.py:15
  66.9 12.3 %collective-permute-start.7 = (f32[384]{0:T(512)S(1)}, f32[384]{0:T(512)S(1)}, u32[]{:S(2)}, u32[]{:S(2)}) collective-permute-start(f32[384]{0:T(512)S(1)} %convert_reduce_fusion), channel_id=1, source_target_pairs={{2,0},{3,1},{4,2},{5,3},{6,4},{7,5},{8,6},{9,7},{10,8},{11,9},{12,... | collective-permute-start | bytes 4616 | tf_op jit(solution)/shard_map/ppermute | solution.py:15
  81.3 6.6 %collective-permute-start.8 = (f32[2,64,256]{2,1,0:T(8,128)S(1)}, f32[2,64,256]{2,1,0:T(8,128)S(1)}, u32[]{:S(2)}, u32[]{:S(2)}) collective-permute-start(f32[2,64,256]{2,1,0:T(8,128)S(1)} %get-tuple-element.128), channel_id=1, source_target_pairs={{0,1},{1,2},{2,3},{3,4},{4,5},{5,6},{6,7},{7,8},{8,9},{9,10},{10,1... | collective-permute-start | bytes 393224 | tf_op jit(solution)/shard_map/ppermute | solution.py:25
  86.0 8.1 %collective-permute-start.9 = (f32[2,64,256]{2,1,0:T(8,128)S(1)}, f32[2,64,256]{2,1,0:T(8,128)S(1)}, u32[]{:S(2)}, u32[]{:S(2)}) collective-permute-start(f32[2,64,256]{2,1,0:T(8,128)S(1)} %get-tuple-element.129), channel_id=1, source_target_pairs={{1,0},{2,1},{3,2},{4,3},{5,4},{6,5},{7,6},{8,7},{9,8},{10,9},{11,1... | collective-permute-start | bytes 393224 | tf_op jit(solution)/shard_map/ppermute | solution.py:26
  97.0 4.4 %collective-permute-start.10 = (f32[2,64,256]{2,1,0:T(8,128)S(1)}, f32[2,64,256]{2,1,0:T(8,128)S(1)}, u32[]{:S(2)}, u32[]{:S(2)}) collective-permute-start(f32[2,64,256]{2,1,0:T(8,128)S(1)} %get-tuple-element.124), channel_id=1, source_target_pairs={{0,1},{1,2},{2,3},{3,4},{4,5},{5,6},{6,7},{7,8},{8,9},{9,10},{10,1... | collective-permute-start | bytes 393224 | tf_op jit(solution)/shard_map/ppermute | solution.py:25
  98.9 8.1 %collective-permute-start.11 = (f32[2,64,256]{2,1,0:T(8,128)S(1)}, f32[2,64,256]{2,1,0:T(8,128)S(1)}, u32[]{:S(2)}, u32[]{:S(2)}) collective-permute-start(f32[2,64,256]{2,1,0:T(8,128)S(1)} %get-tuple-element.125), channel_id=1, source_target_pairs={{1,0},{2,1},{3,2},{4,3},{5,4},{6,5},{7,6},{8,7},{9,8},{10,9},{11,1... | collective-permute-start | bytes 393224 | tf_op jit(solution)/shard_map/ppermute | solution.py:26
where the time goes:
time: 111 us
  waiting for transfers between devices  49.2 us (44%)
  starting transfers between devices  36.5 us (33%)
  between operations  13.2 us (12%)
  other arithmetic  9.57 us (9%)
  local copies, waits for them, and re-layouts  2.35 us (2%)
    ppermute x8, waiting for transfers between devices, passed_along(): return lax.ppermute(block, axis, route)  37.4 us
    ppermute x8, starting transfers between devices, passed_along(): return lax.ppermute(block, axis, route)  25.6 us
    ppermute x2, waiting for transfers between devices, padded_2(): after = lax.ppermute(leading, axis, down)  11.8 us
    ppermute x2, starting transfers between devices, padded_2(): before = lax.ppermute(last, axis, up)  6.55 us
    add x4, other arithmetic, diffuse(): return center + 0.12 * flux_sum  5.02 us
    ppermute x2, starting transfers between devices, padded_2(): after = lax.ppermute(leading, axis, down)  4.33 us
  transfers between devices with their start and end apart: 12, of which 4 were waited for; matrix products, arithmetic and copies ran while one was open for 1% of the time, Pallas kernels for 0%

commit v1 on v0

v1 whole, which is shorter than its diff:
```python
import functools

import jax
import jax.numpy as jnp
from jax import lax
from jax.experimental import pallas as pl
from jax.experimental.pallas import tpu as pltpu
from jax.sharding import PartitionSpec as P

BX = 256
LANES = 128
LEVELS = 32767.0
thresholds = (1.0, 0.8, 0.6, 0.5)
HALO = len(thresholds)
MESH = pl.DeviceIdType.MESH


def window(array, offset):
    shift = (LANES - offset) & (LANES - 1)
    parts = [
        pltpu.roll(array[:, LANES * j : LANES * (j + 1)], shift, 1)
        for j in range(BX // LANES + 1)
    ]
    lane = lax.broadcasted_iota(jnp.int32, parts[0].shape, 1)
    inside = lane < LANES - offset
    return jnp.concatenate(
        [jnp.where(inside, parts[j], parts[j + 1]) for j in range(BX // LANES)], axis=1
    )


def quotient(difference, square):
    bottom = square + difference * difference
    guess = pl.reciprocal(bottom, approx=True)
    return difference * (guess * (2.0 - bottom * guess))


def kernel(
    n, raw, flat, dark, ramp, used, off, out,
    praw, pflat, pdark, pramp, fused, foff, nused, noff,
    corr, pcorr, qf, qn, rf, rn, sf, sn, rsf, rsn, u, send, recv,
):
    depth, rows = raw.shape[0], raw.shape[1]
    half = depth // 2
    me = lax.axis_index("blk")
    s = 2 * lax.rem(me, 2) - 1
    partner, near, far, far_from = me - s, me + s, me + 2 * s, me - 2 * s

    def inside(device):
        return jnp.logical_and(device >= 0, device < n)

    has_near, has_far, has_far_from = inside(near), inside(far), inside(far_from)
    has_below, has_above = me > 0, me < n - 1

    barrier = pltpu.get_barrier_semaphore()

    def greet(device):
        pl.semaphore_signal(barrier, inc=1, device_id=(device,), device_id_type=MESH)

    greet(partner)
    for device, there in ((near, has_near), (far, has_far), (far_from, has_far_from)):
        pl.when(there)(functools.partial(greet, device))
    pl.semaphore_wait(
        barrier,
        1
        + has_near.astype(jnp.int32)
        + has_far.astype(jnp.int32)
        + has_far_from.astype(jnp.int32),
    )

    def copy(number, source, target, device):
        return pltpu.make_async_remote_copy(
            src_ref=source,
            dst_ref=target,
            send_sem=send.at[number],
            recv_sem=recv.at[number],
            device_id=(device,),
            device_id_type=MESH,
        )

    meta_far = [copy(4, used, fused, far_from), copy(5, off, foff, far_from)]
    meta_near = [copy(6, used, nused, near), copy(7, off, noff, near)]
    tile = [
        copy(3, ramp, pramp, partner),
        copy(1, flat, pflat, partner),
        copy(2, dark, pdark, partner),
        copy(0, raw, praw, partner),
    ]

    def part(ref, chunk):
        return ref.at[pl.ds(chunk * half, half)]

    to_far = [copy(8 + c, part(qf, c), part(rf, c), far) for c in range(2)]
    to_far.append(copy(10, sf, rsf, far))
    to_near = [copy(11 + c, part(qn, c), part(rn, c), near) for c in range(2)]
    to_near.append(copy(13, sn, rsn, near))
    down = copy(14, u.at[pl.ds(HALO, HALO)], u.at[pl.ds(HALO + depth, HALO)], me - 1)
    up = copy(15, u.at[pl.ds(depth, HALO)], u.at[pl.ds(0, HALO)], me + 1)

    @pl.when(has_far_from)
    def _():
        for c in meta_far:
            c.start()

    @pl.when(has_near)
    def _():
        for c in meta_near:
            c.start()

    for c in tile:
        c.start()

    def corrected(raw_ref, flat_ref, dark_ref, target):
        inverse = 1.0 / flat_ref[0].astype(jnp.float32)
        level = dark_ref[0].astype(jnp.float32)

        def body(z, largest):
            value = (raw_ref[z].astype(jnp.float32) - level) * inverse
            target[z] = value
            return jnp.maximum(
                largest, jnp.max(jnp.abs(value).reshape(rows // 8, 8, -1), axis=0)
            )

        largest = lax.fori_loop(
            0, depth, body, jnp.zeros((8, raw_ref.shape[2]), jnp.float32)
        )
        return jnp.broadcast_to(
            jnp.max(largest, axis=0, keepdims=True), largest.shape
        )

    def weight(ramp_ref, taken, offset):
        row = jnp.broadcast_to(ramp_ref[...].astype(jnp.float32), (8, ramp_ref.shape[1]))
        return jnp.where(taken == 1, window(row, offset), 0.0)

    def levels(largest):
        return jnp.where(largest > 1e-30, LEVELS / jnp.maximum(largest, 1e-30), 0.0)

    def coded(value):
        return jnp.round(value).astype(jnp.int32).astype(jnp.int16)

    largest = corrected(raw, flat, dark, corr)

    @pl.when(has_far)
    def _():
        for c in meta_far:
            c.wait_recv()
        slot = 2 - 2 * s
        offset = foff[0, slot]
        scale = window(largest, offset)
        w = weight(ramp, fused[0, slot], offset)
        sf[0:8] = w * scale * (1.0 / LEVELS)
        sf[8:16] = w
        to_far[2].start()
        gain = levels(scale)[0:1]
        for c in range(2):
            def body(z, _):
                qf[z] = coded(window(corr[z], offset) * gain)
                return 0

            lax.fori_loop(c * half, (c + 1) * half, body, 0)
            to_far[c].start()

    for c in tile:
        c.wait_recv()
    plargest = corrected(praw, pflat, pdark, pcorr)

    @pl.when(has_near)
    def _():
        for c in meta_near:
            c.wait_recv()
        own, other = 2 - s, 2 - 2 * s
        offset, poffset = noff[0, own], noff[0, other]
        w = weight(ramp, nused[0, own], offset)
        pw = weight(pramp, nused[0, other], poffset)
        total = w + pw
        scale = jnp.maximum(
            jnp.where(w > 0.0, window(largest, offset), 0.0),
            jnp.where(pw > 0.0, window(plargest, poffset), 0.0),
        )
        sn[0:8] = total * scale * (1.0 / LEVELS)
        sn[8:16] = total
        to_near[2].start()
        gain = levels(scale) / jnp.maximum(total, 1.0)
        a, b = (w * gain)[0:1], (pw * gain)[0:1]
        for c in range(2):
            def body(z, _):
                qn[z] = coded(
                    window(corr[z], offset) * a + window(pcorr[z], poffset) * b
                )
                return 0

            lax.fori_loop(c * half, (c + 1) * half, body, 0)
            to_near[c].start()

    offset, poffset = off[0, 2], off[0, 2 - s]
    w = weight(ramp, used[0, 2], offset)
    pw = weight(pramp, used[0, 2 - s], poffset)
    a, b = w[0:1], pw[0:1]

    def base(z, _):
        u[HALO + z] = window(corr[z], offset) * a + window(pcorr[z], poffset) * b
        return 0

    lax.fori_loop(0, depth, base, 0)

    @pl.when(jnp.logical_not(has_far_from))
    def _():
        rsf[...] = jnp.zeros_like(rsf)

    @pl.when(jnp.logical_not(has_near))
    def _():
        rsn[...] = jnp.zeros_like(rsn)

    @pl.when(jnp.logical_not(has_below))
    def _():
        u[0:HALO] = jnp.zeros((HALO,) + u.shape[1:], jnp.float32)

    @pl.when(jnp.logical_not(has_above))
    def _():
        u[HALO + depth :] = jnp.zeros((HALO,) + u.shape[1:], jnp.float32)

    pl.when(has_far_from)(to_far[2].wait_recv)
    pl.when(has_near)(to_near[2].wait_recv)
    inverse = 1.0 / (w + pw + rsf[8:16] + rsn[8:16])
    scale_f = (rsf[0:8] * inverse)[0:1]
    scale_n = (rsn[0:8] * inverse)[0:1]
    inverse = inverse[0:1]
    for c in range(2):
        pl.when(has_far_from)(to_far[c].wait_recv)
        pl.when(has_near)(to_near[c].wait_recv)

        def join(z, _):
            u[HALO + z] = (
                u[HALO + z] * inverse
                + rf[z].astype(jnp.float32) * scale_f
                + rn[z].astype(jnp.float32) * scale_n
            )
            return 0

        lax.fori_loop(c * half, (c + 1) * half, join, 0)
        if c == 0:
            pl.when(has_below)(down.start)
        else:
            pl.when(has_above)(up.start)

    pl.when(has_below)(down.wait_send)
    pl.when(has_above)(up.wait_send)
    pl.when(has_above)(down.wait_recv)
    pl.when(has_below)(up.wait_recv)

    y = lax.broadcasted_iota(jnp.int32, u.shape[1:], 0)
    x = lax.broadcasted_iota(jnp.int32, u.shape[1:], 1)
    for number, kappa in enumerate(thresholds):
        square = kappa * kappa
        first = number + 1
        last = 2 * HALO + depth - 1 - number
        final = number == len(thresholds) - 1

        def body(z, before, square=square, final=final):
            here, following = u[z], u[z + 1]
            closed = jnp.logical_or(
                jnp.logical_and(z == HALO - 1, jnp.logical_not(has_below)),
                jnp.logical_and(z == HALO + depth - 1, jnp.logical_not(has_above)),
            )
            keep = jnp.where(closed, 0.0, 1.0)
            after = quotient((following - here) * keep, square)
            step = pltpu.roll(here, rows - 1, 0) - here
            flow_y = quotient(jnp.where(y == rows - 1, 0.0, step), square)
            step = pltpu.roll(here, BX - 1, 1) - here
            flow_x = quotient(jnp.where(x == BX - 1, 0.0, step), square)
            flux = (
                (after - before)
                + (flow_y - pltpu.roll(flow_y, 1, 0))
                + (flow_x - pltpu.roll(flow_x, 1, 1))
            )
            value = here + (0.12 * square) * flux
            if final:
                out[z - HALO] = value
            else:
                u[z] = value
            return after

        keep = 1.0
        if final:
            keep = jnp.where(has_below, 1.0, 0.0)
        before = quotient((u[first] - u[first - 1]) * keep, square)
        lax.fori_loop(first, last, body, before)

    for c in tile:
        c.wait_send()

    @pl.when(has_far_from)
    def _():
        for c in meta_far:
            c.wait_send()

    @pl.when(has_near)
    def _():
        for c in meta_near + to_near:
            c.wait_send()

    @pl.when(has_far)
    def _():
        for c in to_far:
            c.wait_send()


def shards(raw, flat, dark, ramp, used, off):
    n = lax.axis_size("blk")
    depth, rows, columns = raw.shape
    vmem = pl.BlockSpec(memory_space=pltpu.VMEM)
    smem = pl.BlockSpec(memory_space=pltpu.SMEM)
    coded = pltpu.VMEM((depth, rows, BX), jnp.int16)
    side = pltpu.VMEM((16, BX), jnp.float32)
    tile = pltpu.VMEM(raw.shape, jnp.float32)
    meta = pltpu.SMEM(used.shape, jnp.int32)
    return pl.pallas_call(
        functools.partial(kernel, n),
        out_shape=jax.ShapeDtypeStruct((depth, rows, BX), jnp.float32),
        in_specs=[vmem, vmem, vmem, vmem, smem, smem],
        out_specs=vmem,
        scratch_shapes=[
            pltpu.VMEM(raw.shape, raw.dtype),
            pltpu.VMEM(flat.shape, flat.dtype),
            pltpu.VMEM(dark.shape, dark.dtype),
            pltpu.VMEM(ramp.shape, ramp.dtype),
            meta, meta, meta, meta,
            tile, tile, coded, coded, coded, coded, side, side, side, side,
            pltpu.VMEM((depth + 2 * HALO, rows, BX), jnp.float32),
            pltpu.SemaphoreType.DMA((16,)),
            pltpu.SemaphoreType.DMA((16,)),
        ],
        compiler_params=pltpu.CompilerParams(
            collective_id=0, has_side_effects=True, vmem_limit_bytes=24 * 2**20
        ),
        cost_estimate=pl.CostEstimate(
            flops=30 * 6 * depth * rows * BX, bytes_accessed=10**6, transcendentals=0
        ),
    )(raw, flat, dark, ramp, used, off)


def solution(mesh):
    return jax.shard_map(
        shards,
        mesh=mesh,
        in_specs=(
            P("blk", None, None),
            P("blk", None, None),
            P("blk", None, None),
            P("blk", None),
            P("blk", None),
            P("blk", None),
        ),
        out_specs=P("blk", None, None),
        check_vma=False,
    )
```

time: 111 us -> 42.1 us (0.38)
  the two profiles are of different devices: /device:TPU:7 before, /device:TPU:1 now
where the time goes in v1:
time: 42.1 us; the launch traced here: 41.8 us
  Pallas kernels  36.4 us (86%)
  local copies, waits for them, and re-layouts  5.38 us (13%)
    pallas_call x1, Pallas kernels, shards(): pl.pallas_call(functools.partial(kernel, n), out_shape=jax.ShapeDtypeStru...  36.4 us
    unnamed x13, local copies, waits for them, and re-layouts  5.38 us

profile of v1, /device:TPU:1, one launch (start us, length us, event | category | flops | bytes accessed | tf_op | source)
XLA Modules:
  0.0 41.8 jit_solution(3668688902718617341)
XLA Ops:
  0.0 0.0 copy-start
  0.0 1.0 %copy-done = bf16[8,64,384]{2,1,0:T(8,128)(2,1)S(1)} copy-done((bf16[8,64,384]{2,1,0:T(8,128)(2,1)S(1)}, bf16[8,64,384]{2,1,0:T(8,128)(2,1)}, u32[]{:S(2)}) %copy-start) | copy-done | bytes 393240
  1.0 0.0 copy-start.1
  1.0 0.8 %copy-done.1 = bf16[1,64,384]{2,1,0:T(8,128)(2,1)S(1)} copy-done((bf16[1,64,384]{2,1,0:T(8,128)(2,1)S(1)}, bf16[1,64,384]{2,1,0:T(8,128)(2,1)}, u32[]{:S(2)}) %copy-start.1) | copy-done | bytes 49176
  1.8 0.0 copy-start.2
  1.8 0.8 %copy-done.2 = bf16[1,64,384]{2,1,0:T(8,128)(2,1)S(1)} copy-done((bf16[1,64,384]{2,1,0:T(8,128)(2,1)S(1)}, bf16[1,64,384]{2,1,0:T(8,128)(2,1)}, u32[]{:S(2)}) %copy-start.2) | copy-done | bytes 49176
  2.6 0.0 copy-start.3
  2.6 0.7 %copy-done.3 = s32[1,384]{1,0:T(1,128)S(1)} copy-done((s32[1,384]{1,0:T(1,128)S(1)}, s32[1,384]{1,0:T(1,128)}, u32[]{:S(2)}) %copy-start.3) | copy-done | bytes 1560
  3.3 0.0 copy-start.4
  3.3 0.7 %copy-done.4 = s32[1,5]{1,0:T(1,128)S(1)} copy-done((s32[1,5]{1,0:T(1,128)S(1)}, s32[1,5]{1,0:T(1,128)}, u32[]{:S(2)}) %copy-start.4) | copy-done | bytes 44
  3.9 0.0 copy-start.5
  3.9 0.7 %copy-done.5 = s32[1,5]{1,0:T(1,128)S(1)} copy-done((s32[1,5]{1,0:T(1,128)S(1)}, s32[1,5]{1,0:T(1,128)}, u32[]{:S(2)}) %copy-start.5) | copy-done | bytes 44
  4.6 36.4 %shard_map.64 = f32[8,64,256]{2,1,0:T(8,128)S(1)} custom-call(bf16[8,64,384]{2,1,0:T(8,128)(2,1)S(1)} %copy-done, bf16[1,64,384]{2,1,0:T(8,128)(2,1)S(1)} %copy-done.1, bf16[1,64,384]{2,1,0:T(8,128)(2,1)S(1)} %copy-done.2, s32[1,384]{1,0:T(1,128)S(1)} %copy-done.3, s32[1,5]{1,0:T(1,128)S(1)} %copy-done.4, s32[1,5]{1,0:T(1,128)S(1)} %copy-done.5), custom_call_target="tpu_custom_call" | custom-call | flops 23592960 | bytes 1000000 | tf_op jit(solution)/shard_map/pallas_call | solution.py:316
  41.0 0.8 %copy.8 = f32[8,64,256]{2,1,0:T(8,128)} copy(f32[8,64,256]{2,1,0:T(8,128)S(1)} %shard_map.64) | data formatting | bytes 1048576
Async XLA Ops:
  0.0 1.0 %copy-start = (bf16[8,64,384]{2,1,0:T(8,128)(2,1)S(1)}, bf16[8,64,384]{2,1,0:T(8,128)(2,1)}, u32[]{:S(2)}) copy-start(bf16[8,64,384]{2,1,0:T(8,128)(2,1)} %raw.1) | copy-start | bytes 1179652
  1.0 0.8 %copy-start.1 = (bf16[1,64,384]{2,1,0:T(8,128)(2,1)S(1)}, bf16[1,64,384]{2,1,0:T(8,128)(2,1)}, u32[]{:S(2)}) copy-start(bf16[1,64,384]{2,1,0:T(8,128)(2,1)} %flat.1) | copy-start | bytes 147460
  1.8 0.8 %copy-start.2 = (bf16[1,64,384]{2,1,0:T(8,128)(2,1)S(1)}, bf16[1,64,384]{2,1,0:T(8,128)(2,1)}, u32[]{:S(2)}) copy-start(bf16[1,64,384]{2,1,0:T(8,128)(2,1)} %dark.1) | copy-start | bytes 147460
  2.6 0.7 %copy-start.3 = (s32[1,384]{1,0:T(1,128)S(1)}, s32[1,384]{1,0:T(1,128)}, u32[]{:S(2)}) copy-start(s32[1,384]{1,0:T(1,128)} %ramp.1) | copy-start | bytes 4612
  3.3 0.7 %copy-start.4 = (s32[1,5]{1,0:T(1,128)S(1)}, s32[1,5]{1,0:T(1,128)}, u32[]{:S(2)}) copy-start(s32[1,5]{1,0:T(1,128)} %used.1) | copy-start | bytes 64
  3.9 0.7 %copy-start.5 = (s32[1,5]{1,0:T(1,128)S(1)}, s32[1,5]{1,0:T(1,128)}, u32[]{:S(2)}) copy-start(s32[1,5]{1,0:T(1,128)} %off.1) | copy-start | bytes 64

commit v2 on v1

--- a/solution.py
+++ b/solution.py
@@ -35,9 +35,11 @@
 
 
 def kernel(
-    n, raw, flat, dark, ramp, used, off, out,
+    n, graw, gflat, gdark, gramp, gused, goff, out,
+    raw, flat, dark, ramp, used, off,
     praw, pflat, pdark, pramp, fused, foff, nused, noff,
-    corr, pcorr, qf, qn, rf, rn, sf, sn, rsf, rsn, u, send, recv,
+    corr, pcorr, qf, qn, rf, rn, sf, sn, rsf, rsn,
+    qh, rh, sh, rsh, saved, u, local, send, recv,
 ):
     depth, rows = raw.shape[0], raw.shape[1]
     half = depth // 2
@@ -50,6 +52,15 @@
 
     has_near, has_far, has_far_from = inside(near), inside(far), inside(far_from)
     has_below, has_above = me > 0, me < n - 1
+
+    fetched = [
+        pltpu.make_async_copy(source, target, local.at[number])
+        for number, (source, target) in enumerate(
+            ((gflat, flat), (gdark, dark), (graw, raw), (gramp, ramp), (gused, used), (goff, off))
+        )
+    ]
+    for c in fetched:
+        c.start()
 
     barrier = pltpu.get_barrier_semaphore()
 
@@ -77,13 +88,13 @@
             device_id_type=MESH,
         )
 
-    meta_far = [copy(4, used, fused, far_from), copy(5, off, foff, far_from)]
-    meta_near = [copy(6, used, nused, near), copy(7, off, noff, near)]
+    meta_far = [copy(4, gused, fused, far_from), copy(5, goff, foff, far_from)]
+    meta_near = [copy(6, gused, nused, near), copy(7, goff, noff, near)]
     tile = [
-        copy(3, ramp, pramp, partner),
-        copy(1, flat, pflat, partner),
-        copy(2, dark, pdark, partner),
-        copy(0, raw, praw, partner),
+        copy(3, gramp, pramp, partner),
+        copy(1, gflat, pflat, partner),
+        copy(2, gdark, pdark, partner),
+        copy(0, graw, praw, partner),
     ]
 
     def part(ref, chunk):
@@ -93,8 +104,10 @@
     to_far.append(copy(10, sf, rsf, far))
     to_near = [copy(11 + c, part(qn, c), part(rn, c), near) for c in range(2)]
     to_near.append(copy(13, sn, rsn, near))
-    down = copy(14, u.at[pl.ds(HALO, HALO)], u.at[pl.ds(HALO + depth, HALO)], me - 1)
-    up = copy(15, u.at[pl.ds(depth, HALO)], u.at[pl.ds(0, HALO)], me + 1)
+    halos = [
+        [copy(14, qh.at[0], rh.at[1], me - 1), copy(15, sh.at[0], rsh.at[1], me - 1)],
+        [copy(16, qh.at[1], rh.at[0], me + 1), copy(17, sh.at[1], rsh.at[0], me + 1)],
+    ]
 
     @pl.when(has_far_from)
     def _():
@@ -137,6 +150,8 @@
     def coded(value):
         return jnp.round(value).astype(jnp.int32).astype(jnp.int16)
 
+    for c in fetched:
+        c.wait()
     largest = corrected(raw, flat, dark, corr)
 
     @pl.when(has_far)
@@ -228,62 +243,133 @@
         pl.when(has_far_from)(to_far[c].wait_recv)
         pl.when(has_near)(to_near[c].wait_recv)
 
-        def join(z, _):
-            u[HALO + z] = (
+        def join(z, largest):
+            value = (
                 u[HALO + z] * inverse
                 + rf[z].astype(jnp.float32) * scale_f
                 + rn[z].astype(jnp.float32) * scale_n
             )
-            return 0
-
-        lax.fori_loop(c * half, (c + 1) * half, join, 0)
-        if c == 0:
-            pl.when(has_below)(down.start)
-        else:
-            pl.when(has_above)(up.start)
-
-    pl.when(has_below)(down.wait_send)
-    pl.when(has_above)(up.wait_send)
-    pl.when(has_above)(down.wait_recv)
-    pl.when(has_below)(up.wait_recv)
+            u[HALO + z] = value
+            return jnp.maximum(
+                largest, jnp.max(jnp.abs(value).reshape(rows // 8, 8, -1), axis=0)
+            )
+
+        largest = lax.fori_loop(
+            c * half, (c + 1) * half, join, jnp.zeros((8, BX), jnp.float32)
+        )
+
+        @pl.when((has_below, has_above)[c])
+        def _():
+            scale = jnp.max(largest, axis=0, keepdims=True)
+            sh[c] = jnp.broadcast_to(scale * (1.0 / LEVELS), (8, BX))
+            gain = levels(scale)
+            start = c * (depth - HALO)
+
+            def code(z, _):
+                qh[c, z] = coded(u[HALO + start + z] * gain)
+                return 0
+
+            lax.fori_loop(0, HALO, code, 0)
+            for halo in halos[c]:
+                halo.start()
 
     y = lax.broadcasted_iota(jnp.int32, u.shape[1:], 0)
     x = lax.broadcasted_iota(jnp.int32, u.shape[1:], 1)
+
+    def stepped(here, before, after, square):
+        step = pltpu.roll(here, rows - 1, 0) - here
+        flow_y = quotient(jnp.where(y == rows - 1, 0.0, step), square)
+        step = pltpu.roll(here, BX - 1, 1) - here
+        flow_x = quotient(jnp.where(x == BX - 1, 0.0, step), square)
+        flux = (
+            (after - before)
+            + (flow_y - pltpu.roll(flow_y, 1, 0))
+            + (flow_x - pltpu.roll(flow_x, 1, 1))
+        )
+        return here + (0.12 * square) * flux
+
+    planes = depth + 2 * HALO
     for number, kappa in enumerate(thresholds):
         square = kappa * kappa
-        first = number + 1
-        last = 2 * HALO + depth - 1 - number
-        final = number == len(thresholds) - 1
-
-        def body(z, before, square=square, final=final):
-            here, following = u[z], u[z + 1]
-            closed = jnp.logical_or(
-                jnp.logical_and(z == HALO - 1, jnp.logical_not(has_below)),
-                jnp.logical_and(z == HALO + depth - 1, jnp.logical_not(has_above)),
+        first, last = HALO + 1 + number, planes - HALO - 1 - number
+
+        def body(z, before, square=square):
+            here = u[z]
+            after = quotient(u[z + 1] - here, square)
+            u[z] = stepped(here, before, after, square)
+            return after
+
+        before = quotient(u[first] - u[first - 1], square)
+        saved[0, number] = before
+        saved[1, number] = -lax.fori_loop(first, last, body, before)
+
+    lower_first = s > 0
+    for turn in range(2):
+        lower = lower_first if turn == 0 else jnp.logical_not(lower_first)
+        side = jnp.where(lower, 0, 1)
+        there = jnp.where(lower, has_below, has_above)
+        origin = side * (planes - 1)
+        sign = 1 - 2 * side
+
+        @pl.when(jnp.logical_and(lower, has_below))
+        def _():
+            for halo in halos[1]:
+                halo.wait_recv()
+
+        @pl.when(jnp.logical_and(jnp.logical_not(lower), has_above))
+        def _():
+            for halo in halos[0]:
+                halo.wait_recv()
+
+        @pl.when(there)
+        def _():
+            scale = rsh[side, 0:1]
+
+            def decode(z, _):
+                u[side * (HALO + depth) + z] = rh[side, z].astype(jnp.float32) * scale
+                return 0
+
+            lax.fori_loop(0, HALO, decode, 0)
+
+        open_face = jnp.where(there, 1.0, 0.0)
+        for number, kappa in enumerate(thresholds):
+            square = kappa * kappa
+            final = number == HALO - 1
+
+            def store(k, value, final=final):
+                if final:
+                    out[origin + sign * k - HALO] = value
+                else:
+                    u[origin + sign * k] = value
+
+            def between(k, square=square):
+                keep = jnp.where(k == HALO - 1, open_face, 1.0)
+                return quotient(
+                    (u[origin + sign * (k + 1)] - u[origin + sign * k]) * keep, square
+                )
+
+            def body(k, before, square=square, store=store, between=between):
+                after = between(k)
+                store(k, stepped(u[origin + sign * k], before, after, square))
+                return after
+
+            before = lax.fori_loop(
+                number + 1, number + HALO, body, between(jnp.int32(number))
             )
-            keep = jnp.where(closed, 0.0, 1.0)
-            after = quotient((following - here) * keep, square)
-            step = pltpu.roll(here, rows - 1, 0) - here
-            flow_y = quotient(jnp.where(y == rows - 1, 0.0, step), square)
-            step = pltpu.roll(here, BX - 1, 1) - here
-            flow_x = quotient(jnp.where(x == BX - 1, 0.0, step), square)
-            flux = (
-                (after - before)
-                + (flow_y - pltpu.roll(flow_y, 1, 0))
-                + (flow_x - pltpu.roll(flow_x, 1, 1))
+            k = number + HALO
+            store(
+                k, stepped(u[origin + sign * k], before, saved[side, number], square)
             )
-            value = here + (0.12 * square) * flux
-            if final:
-                out[z - HALO] = value
-            else:
-                u[z] = value
-            return after
-
-        keep = 1.0
-        if final:
-            keep = jnp.where(has_below, 1.0, 0.0)
-        before = quotient((u[first] - u[first - 1]) * keep, square)
-        lax.fori_loop(first, last, body, before)
+
+    @pl.when(has_below)
+    def _():
+        for halo in halos[0]:
+            halo.wait_send()
+
+    @pl.when(has_above)
+    def _():
+        for halo in halos[1]:
+            halo.wait_send()
 
     for c in tile:
         c.wait_send()
@@ -308,29 +394,31 @@
     n = lax.axis_size("blk")
     depth, rows, columns = raw.shape
     vmem = pl.BlockSpec(memory_space=pltpu.VMEM)
-    smem = pl.BlockSpec(memory_space=pltpu.SMEM)
     coded = pltpu.VMEM((depth, rows, BX), jnp.int16)
     side = pltpu.VMEM((16, BX), jnp.float32)
     tile = pltpu.VMEM(raw.shape, jnp.float32)
     meta = pltpu.SMEM(used.shape, jnp.int32)
+    held = [pltpu.VMEM(a.shape, a.dtype) for a in (raw, flat, dark, ramp)]
     return pl.pallas_call(
         functools.partial(kernel, n),
         out_shape=jax.ShapeDtypeStruct((depth, rows, BX), jnp.float32),
-        in_specs=[vmem, vmem, vmem, vmem, smem, smem],
+        in_specs=[pl.BlockSpec(memory_space=pl.ANY)] * 6,
         out_specs=vmem,
         scratch_shapes=[
-            pltpu.VMEM(raw.shape, raw.dtype),
-            pltpu.VMEM(flat.shape, flat.dtype),
-            pltpu.VMEM(dark.shape, dark.dtype),
-            pltpu.VMEM(ramp.shape, ramp.dtype),
-            meta, meta, meta, meta,
+            *held, meta, meta, *held, meta, meta, meta, meta,
             tile, tile, coded, coded, coded, coded, side, side, side, side,
+            pltpu.VMEM((2, HALO, rows, BX), jnp.int16),
+            pltpu.VMEM((2, HALO, rows, BX), jnp.int16),
+            pltpu.VMEM((2, 8, BX), jnp.float32),
+            pltpu.VMEM((2, 8, BX), jnp.float32),
+            pltpu.VMEM((2, len(thresholds), rows, BX), jnp.float32),
             pltpu.VMEM((depth + 2 * HALO, rows, BX), jnp.float32),
-            pltpu.SemaphoreType.DMA((16,)),
-            pltpu.SemaphoreType.DMA((16,)),
+            pltpu.SemaphoreType.DMA((6,)),
+            pltpu.SemaphoreType.DMA((18,)),
+            pltpu.SemaphoreType.DMA((18,)),
         ],
         compiler_params=pltpu.CompilerParams(
-            collective_id=0, has_side_effects=True, vmem_limit_bytes=24 * 2**20
+            collective_id=0, has_side_effects=True, vmem_limit_bytes=64 * 2**20 - 2**17
         ),
         cost_estimate=pl.CostEstimate(
             flops=30 * 6 * depth * rows * BX, bytes_accessed=10**6, transcendentals=0

time: 42.1 us -> 32.1 us (0.76)
  the two profiles are of different devices: /device:TPU:1 before, /device:TPU:29 now
where the time goes in v2:
time: 32.1 us; the launch traced here: 31.9 us
  Pallas kernels  30 us (93%)
  local copies, waits for them, and re-layouts  1.87 us (6%)
    pallas_call x1, Pallas kernels, shards(): pl.pallas_call(functools.partial(kernel, n), out_shape=jax.ShapeDtypeStru...  30 us
    unnamed x1, local copies, waits for them, and re-layouts  1.87 us

profile of v2, /device:TPU:29, one launch (start us, length us, event | category | flops | bytes accessed | tf_op | source)
XLA Modules:
  0.0 31.9 jit_solution(3891443927364917622)
XLA Ops:
  0.0 30.0 %shard_map.64 = f32[8,64,256]{2,1,0:T(8,128)} custom-call(bf16[8,64,384]{2,1,0:T(8,128)(2,1)} %graw.1, bf16[1,64,384]{2,1,0:T(8,128)(2,1)} %gflat.1, bf16[1,64,384]{2,1,0:T(8,128)(2,1)} %gdark.1, s32[1,384]{1,0:T(1,128)} %gramp.1, s32[1,5]{1,0:T(1,128)} %gused.1, s32[1,5]{1,0:T(1,128)} %goff.1), custom_call_target="tpu_custom_call" | custom-call | flops 23592960 | bytes 1000000 | tf_op jit(solution)/shard_map/pallas_call | solution.py:402
  30.0 1.9 %copy.8 = f32[8,64,256]{2,1,0:T(8,128)} copy(f32[8,64,256]{2,1,0:T(8,128)} %shard_map.64) | data formatting | bytes 1048576

commit v3 on v2

--- a/solution.py
+++ b/solution.py
@@ -154,34 +154,31 @@
         c.wait()
     largest = corrected(raw, flat, dark, corr)
 
-    @pl.when(has_far)
-    def _():
-        for c in meta_far:
-            c.wait_recv()
+    def send_far(c):
+        if c == 0:
+            for received in meta_far:
+                received.wait_recv()
         slot = 2 - 2 * s
         offset = foff[0, slot]
         scale = window(largest, offset)
-        w = weight(ramp, fused[0, slot], offset)
-        sf[0:8] = w * scale * (1.0 / LEVELS)
-        sf[8:16] = w
-        to_far[2].start()
+        if c == 0:
+            w = weight(ramp, fused[0, slot], offset)
+            sf[0:8] = w * scale * (1.0 / LEVELS)
+            sf[8:16] = w
+            to_far[2].start()
         gain = levels(scale)[0:1]
-        for c in range(2):
-            def body(z, _):
-                qf[z] = coded(window(corr[z], offset) * gain)
-                return 0
-
-            lax.fori_loop(c * half, (c + 1) * half, body, 0)
-            to_far[c].start()
-
-    for c in tile:
-        c.wait_recv()
-    plargest = corrected(praw, pflat, pdark, pcorr)
-
-    @pl.when(has_near)
-    def _():
-        for c in meta_near:
-            c.wait_recv()
+
+        def body(z, _):
+            qf[z] = coded(window(corr[z], offset) * gain)
+            return 0
+
+        lax.fori_loop(c * half, (c + 1) * half, body, 0)
+        to_far[c].start()
+
+    def send_near(c):
+        if c == 0:
+            for received in meta_near:
+                received.wait_recv()
         own, other = 2 - s, 2 - 2 * s
         offset, poffset = noff[0, own], noff[0, other]
         w = weight(ramp, nused[0, own], offset)
@@ -191,20 +188,31 @@
             jnp.where(w > 0.0, window(largest, offset), 0.0),
             jnp.where(pw > 0.0, window(plargest, poffset), 0.0),
         )
-        sn[0:8] = total * scale * (1.0 / LEVELS)
-        sn[8:16] = total
-        to_near[2].start()
+        if c == 0:
+            sn[0:8] = total * scale * (1.0 / LEVELS)
+            sn[8:16] = total
+            to_near[2].start()
         gain = levels(scale) / jnp.maximum(total, 1.0)
         a, b = (w * gain)[0:1], (pw * gain)[0:1]
-        for c in range(2):
-            def body(z, _):
-                qn[z] = coded(
-                    window(corr[z], offset) * a + window(pcorr[z], poffset) * b
-                )
-                return 0
-
-            lax.fori_loop(c * half, (c + 1) * half, body, 0)
-            to_near[c].start()
+
+        def body(z, _):
+            qn[z] = coded(
+                window(corr[z], offset) * a + window(pcorr[z], poffset) * b
+            )
+            return 0
+
+        lax.fori_loop(c * half, (c + 1) * half, body, 0)
+        to_near[c].start()
+
+    pl.when(has_far)(functools.partial(send_far, 0))
+    for c in tile:
+        c.wait_recv()
+    plargest = corrected(praw, pflat, pdark, pcorr)
+
+    for c in range(2):
+        pl.when(has_near)(functools.partial(send_near, c))
+        if c == 0:
+            pl.when(has_far)(functools.partial(send_far, 1))
 
     offset, poffset = off[0, 2], off[0, 2 - s]
     w = weight(ramp, used[0, 2], offset)
@@ -301,7 +309,9 @@
 
         before = quotient(u[first] - u[first - 1], square)
         saved[0, number] = before
-        saved[1, number] = -lax.fori_loop(first, last, body, before)
+        saved[1, number] = -lax.fori_loop(
+            first, last, body, before, unroll=True
+        )
 
     lower_first = s > 0
     for turn in range(2):
@@ -342,24 +352,20 @@
                 else:
                     u[origin + sign * k] = value
 
-            def between(k, square=square):
-                keep = jnp.where(k == HALO - 1, open_face, 1.0)
-                return quotient(
-                    (u[origin + sign * (k + 1)] - u[origin + sign * k]) * keep, square
-                )
-
-            def body(k, before, square=square, store=store, between=between):
-                after = between(k)
-                store(k, stepped(u[origin + sign * k], before, after, square))
-                return after
-
-            before = lax.fori_loop(
-                number + 1, number + HALO, body, between(jnp.int32(number))
-            )
-            k = number + HALO
-            store(
-                k, stepped(u[origin + sign * k], before, saved[side, number], square)
-            )
+            def between(k, here, following, square=square):
+                step = following - here
+                return quotient(step * open_face if k == HALO - 1 else step, square)
+
+            read = [u[origin + sign * (number + j)] for j in range(HALO + 1)]
+            flows = [
+                between(number + j, read[j], read[j + 1]) for j in range(HALO)
+            ] + [saved[side, number]]
+            values = [
+                stepped(read[j], flows[j - 1], flows[j], square)
+                for j in range(1, HALO + 1)
+            ]
+            for j, value in enumerate(values):
+                store(number + 1 + j, value)
 
     @pl.when(has_below)
     def _():

time: 32.1 us -> 28.5 us (0.89)
  Pallas kernels: 30 us -> 26.5 us
    pallas_call x1, Pallas kernels: 30 us -> 26.5 us  [shards(): pl.pallas_call(functools.partial(kernel, n), out_shape=jax.ShapeDtypeStru...]
where the time goes in v3:
time: 28.5 us; the launch traced here: 28.3 us
  Pallas kernels  26.5 us (93%)
  local copies, waits for them, and re-layouts  1.87 us (7%)
    pallas_call x1, Pallas kernels, shards(): pl.pallas_call(functools.partial(kernel, n), out_shape=jax.ShapeDtypeStru...  26.5 us
    unnamed x1, local copies, waits for them, and re-layouts  1.87 us

profile of v3, /device:TPU:29, one launch (start us, length us, event | category | flops | bytes accessed | tf_op | source)
XLA Modules:
  0.0 28.3 jit_solution(9347347675063331336)
XLA Ops:
  0.0 26.5 %shard_map.64 = f32[8,64,256]{2,1,0:T(8,128)} custom-call(bf16[8,64,384]{2,1,0:T(8,128)(2,1)} %graw.1, bf16[1,64,384]{2,1,0:T(8,128)(2,1)} %gflat.1, bf16[1,64,384]{2,1,0:T(8,128)(2,1)} %gdark.1, s32[1,384]{1,0:T(1,128)} %gramp.1, s32[1,5]{1,0:T(1,128)} %gused.1, s32[1,5]{1,0:T(1,128)} %goff.1), custom_call_target="tpu_custom_call" | custom-call | flops 23592960 | bytes 1000000 | tf_op jit(solution)/shard_map/pallas_call | solution.py:408
  26.5 1.9 %copy.8 = f32[8,64,256]{2,1,0:T(8,128)} copy(f32[8,64,256]{2,1,0:T(8,128)} %shard_map.64) | data formatting | bytes 1048576

commit v4 on v3

--- a/solution.py
+++ b/solution.py
@@ -172,7 +172,7 @@
             qf[z] = coded(window(corr[z], offset) * gain)
             return 0
 
-        lax.fori_loop(c * half, (c + 1) * half, body, 0)
+        lax.fori_loop(c * half, (c + 1) * half, body, 0, unroll=2)
         to_far[c].start()
 
     def send_near(c):
@@ -201,7 +201,7 @@
             )
             return 0
 
-        lax.fori_loop(c * half, (c + 1) * half, body, 0)
+        lax.fori_loop(c * half, (c + 1) * half, body, 0, unroll=2)
         to_near[c].start()
 
     pl.when(has_far)(functools.partial(send_far, 0))
@@ -223,7 +223,7 @@
         u[HALO + z] = window(corr[z], offset) * a + window(pcorr[z], poffset) * b
         return 0
 
-    lax.fori_loop(0, depth, base, 0)
+    lax.fori_loop(0, depth, base, 0, unroll=2)
 
     @pl.when(jnp.logical_not(has_far_from))
     def _():

time: 28.5 us -> 28.4 us (level)
  no operation moved by 1% of the time
where the time goes in v4:
time: 28.4 us; the launch traced here: 28.2 us
  Pallas kernels  26.3 us (93%)
  local copies, waits for them, and re-layouts  1.87 us (7%)
    pallas_call x1, Pallas kernels, shards(): pl.pallas_call(functools.partial(kernel, n), out_shape=jax.ShapeDtypeStru...  26.3 us
    unnamed x1, local copies, waits for them, and re-layouts  1.87 us

profile of v4, /device:TPU:29, one launch (start us, length us, event | category | flops | bytes accessed | tf_op | source)
XLA Modules:
  0.0 28.2 jit_solution(6752160093181972965)
XLA Ops:
  0.0 26.3 %shard_map.64 = f32[8,64,256]{2,1,0:T(8,128)} custom-call(bf16[8,64,384]{2,1,0:T(8,128)(2,1)} %graw.1, bf16[1,64,384]{2,1,0:T(8,128)(2,1)} %gflat.1, bf16[1,64,384]{2,1,0:T(8,128)(2,1)} %gdark.1, s32[1,384]{1,0:T(1,128)} %gramp.1, s32[1,5]{1,0:T(1,128)} %gused.1, s32[1,5]{1,0:T(1,128)} %goff.1), custom_call_target="tpu_custom_call" | custom-call | flops 23592960 | bytes 1000000 | tf_op jit(solution)/shard_map/pallas_call | solution.py:408
  26.3 1.9 %copy.8 = f32[8,64,256]{2,1,0:T(8,128)} copy(f32[8,64,256]{2,1,0:T(8,128)} %shard_map.64) | data formatting | bytes 1048576
